TPU v7x, 32 devices: a whole 2x2x4 slice. The times are simulated.
32 devices in a mesh: sub: 8 (over z, x), tile: 4 (over y, core).
Axes of the slice: x: 2, y: 2, z: 4, core: 2. Of those that a mesh axis runs over, the one named last changes fastest.
Arguments:
- echoes: bfloat16 [2, 4096, 4096], P(None, 'sub', 'tile'), may hold values from -6 to 6
- image: float32 [2, 256, 128, 128], P(None, ('sub', 'tile')), may hold values from -6 to 6
- merge_own: bfloat16 [3, 2, 4096, 128], P(None, None, 'sub'), may hold values from -0.25 to 0.25
- merge_pair: bfloat16 [3, 2, 4096, 128], P(None, None, 'sub'), may hold values from -0.25 to 0.25
- merge_angle: float32 [3, 4096], P(None, 'sub'), may hold values from -3.140625 to 3.140625
- beam_kernel: bfloat16 [128, 128], replicated, may hold values from -0.5 to 0.5
- range_kernel: bfloat16 [128, 128], replicated, may hold values from -0.5 to 0.5
- block_map: int32 [32, 32, 2], P('sub', 'tile'), may hold values from 0 to 31, as said below
- route_angle: float32 [32, 32, 2], P('sub', 'tile'), may hold values from -3.140625 to 3.140625
Outputs:
- new_image: float32 [2, 256, 128, 128], P(None, ('sub', 'tile'))
- residual: bfloat16 [2, 4096, 4096], P(None, 'sub', 'tile')
Inputs may be any that keep to these rules, and one draw needn't show every extreme that they name: `block_map`: each entry names one of the 32 image tiles of the polar tile's own beam sector, counted from the sector's first tile; every tile of every sector is named at least once.
All inputs are finite; a program needn't handle non-finite values.
Results may differ from a plain program's by a relative error of at most 0.017.
Values may be sent and summed in bfloat16 or wider, within the bound.
A program may use at most 64 MiB of HBM per device.

v0:
```python
import jax
import jax.numpy as jnp
from jax import lax
from jax.sharding import PartitionSpec as P

highest = lax.Precision.HIGHEST
step_length = 0.1


def from_partner(block, axis, bit):
    count = lax.axis_size(axis)
    route = []
    for low in range(count):
        high = low | 1 << bit
        if high != low and high < count:
            route += [(low, high), (high, low)]
    return lax.ppermute(block, axis, route)


def blockwise(matrix, field, adjoint):
    block_side = matrix.shape[-1]
    block_count = matrix.shape[1] // block_side
    blocks = matrix.reshape(2, block_count, block_side, block_side)
    values = field.reshape(2, block_count, block_side, field.shape[2])
    pattern = "nac,nar->ncr" if adjoint else "nac,ncr->nar"

    def multiply(left_op, right_op):
        return jnp.einsum(pattern, left_op, right_op, preferred_element_type=jnp.float32)

    real_real = multiply(blocks[0], values[0])
    imag_imag = multiply(blocks[1], values[1])
    real_imag = multiply(blocks[0], values[1])
    imag_real = multiply(blocks[1], values[0])
    if adjoint:
        real_out, imag_out = (real_real + imag_imag, real_imag - imag_real)
    else:
        real_out, imag_out = (real_real - imag_imag, real_imag + imag_real)
    rows_all = field.shape[1]
    return jnp.stack([real_out.reshape(rows_all, -1), imag_out.reshape(rows_all, -1)])


def to_tiles(field, block_side):
    shaped = field.reshape(
        2, field.shape[1] // block_side, block_side, field.shape[2] // block_side, block_side
    )
    return shaped.transpose(0, 1, 3, 2, 4)


def from_tiles(tiles):
    shaped = tiles.transpose(0, 1, 3, 2, 4)
    return shaped.reshape(2, tiles.shape[1] * tiles.shape[3], tiles.shape[2] * tiles.shape[4])


def route_weights(targets, flat_map, flat_cos, flat_sin):
    matched = (flat_map[None, :, :] == targets[:, None, None]).astype(jnp.float32)
    return (jnp.sum(matched * flat_cos[None], axis=2), jnp.sum(matched * flat_sin[None], axis=2))


def per_device(
    echoes,
    image,
    merge_own,
    merge_pair,
    merge_angle,
    beam_kernel,
    range_kernel,
    block_map,
    route_angle,
):
    block_side = beam_kernel.shape[0]
    sections = merge_own.shape[0]
    hits_count = block_map.shape[2]
    range_cols = echoes.shape[2]
    owned_tiles = image.shape[1]
    tile_count = lax.axis_size("tile")
    tile_index = lax.axis_index("tile")
    total_range = range_cols * tile_count
    rho = (
        (tile_index * range_cols + jnp.arange(range_cols)).astype(jnp.float32) + 0.5
    ) / total_range
    phase_list = []
    for section in range(sections):
        theta = merge_angle[section][:, None] * rho[None, :]
        phase_list.append((jnp.cos(theta), jnp.sin(theta)))
    route_cos = jnp.cos(route_angle)
    route_sin = jnp.sin(route_angle)
    image_half = image.astype(jnp.bfloat16)
    region = lax.all_gather(image_half, "tile", axis=1, tiled=True)
    picked = jnp.take(region, block_map, axis=1).astype(jnp.float32)
    cos_full = route_cos[:, :, :, None, None]
    sin_full = route_sin[:, :, :, None, None]
    routed_real = jnp.sum(cos_full * picked[0] + sin_full * picked[1], axis=2)
    routed_imag = jnp.sum(cos_full * picked[1] - sin_full * picked[0], axis=2)
    routed = jnp.stack([routed_real, routed_imag]).astype(jnp.bfloat16)
    half_forward = jnp.einsum(
        "pijac,dc->pijad", routed, range_kernel, preferred_element_type=jnp.float32
    ).astype(jnp.bfloat16)
    polar = jnp.einsum(
        "ka,pijkd->pijad", beam_kernel, half_forward, preferred_element_type=jnp.float32
    ).astype(jnp.bfloat16)
    level = from_tiles(polar)
    for section in reversed(range(sections)):
        phase_cos, phase_sin = phase_list[section]
        level_f = level.astype(jnp.float32)
        turned = jnp.stack(
            [
                phase_cos * level_f[0] + phase_sin * level_f[1],
                phase_cos * level_f[1] - phase_sin * level_f[0],
            ]
        ).astype(jnp.bfloat16)
        own_part = blockwise(merge_own[section], turned, True)
        pair_part = blockwise(merge_pair[section], turned, True).astype(jnp.bfloat16)
        returned = from_partner(pair_part, "sub", section)
        level = (own_part + returned.astype(jnp.float32)).astype(jnp.bfloat16)
    residual = (level.astype(jnp.float32) - echoes.astype(jnp.float32)).astype(jnp.bfloat16)
    field = residual
    for section in range(sections):
        partner = from_partner(field, "sub", section)
        phase_cos, phase_sin = phase_list[section]
        mixed = blockwise(merge_own[section], field, False) + blockwise(
            merge_pair[section], partner, False
        )
        field = jnp.stack(
            [
                phase_cos * mixed[0] - phase_sin * mixed[1],
                phase_cos * mixed[1] + phase_sin * mixed[0],
            ]
        ).astype(jnp.bfloat16)
    tiles = to_tiles(field, block_side)
    beamed = jnp.einsum(
        "ak,pijkc->pijac", beam_kernel, tiles, preferred_element_type=jnp.float32
    ).astype(jnp.bfloat16)
    spread = jnp.einsum(
        "pijac,cd->ijpad", beamed, range_kernel, preferred_element_type=jnp.float32
    ).astype(jnp.bfloat16)
    polar_count = spread.shape[0] * spread.shape[1]
    spread_rows = spread.reshape(polar_count, 2, block_side * block_side)
    flat_map = block_map.reshape(polar_count, hits_count)
    flat_cos = route_cos.reshape(polar_count, hits_count)
    flat_sin = route_sin.reshape(polar_count, hits_count)
    spread_f = spread_rows.astype(jnp.float32)
    targets = jnp.arange(lax.axis_size("tile") * owned_tiles)
    weight_cos, weight_sin = route_weights(targets, flat_map, flat_cos, flat_sin)
    real_sum = jnp.dot(weight_cos, spread_f[:, 0], precision=highest) - jnp.dot(
        weight_sin, spread_f[:, 1], precision=highest
    )
    imag_sum = jnp.dot(weight_cos, spread_f[:, 1], precision=highest) + jnp.dot(
        weight_sin, spread_f[:, 0], precision=highest
    )
    owned = lax.psum_scatter(
        jnp.stack([real_sum, imag_sum], axis=1).astype(jnp.bfloat16),
        "tile",
        scatter_dimension=0,
        tiled=True,
    ).astype(jnp.float32)
    gradient = owned.transpose(1, 0, 2).reshape(2, owned_tiles, block_side, block_side)
    new_image = image - step_length * gradient
    return (new_image, residual)


def solution(mesh):
    return jax.shard_map(
        per_device,
        mesh=mesh,
        in_specs=(
            P(None, "sub", "tile"),
            P(None, ("sub", "tile"), None, None),
            P(None, None, "sub", None),
            P(None, None, "sub", None),
            P(None, "sub"),
            P(),
            P(),
            P("sub", "tile", None),
            P("sub", "tile", None),
        ),
        out_specs=(P(None, ("sub", "tile"), None, None), P(None, "sub", "tile")),
        check_vma=False,
    )
```

profile of v0, /device:TPU:0, one launch (start us, length us, event | category | flops | bytes accessed | tf_op | source)
XLA Modules:
  0.0 557.8 jit_solution(1671828342887338187)
XLA Ops:
  7.3 2.2 convert_element_type.91
  10.2 25.3 %all-gather.2.cloned.1.call-done = bf16[2,32,128,128]{3,2,1,0:T(8,128)(2,1)} async-done(((bf16[2,8,128,128]{3,2,1,0:T(8,128)(2,1)}), bf16[2,32,128,128]{3,2,1,0:T(8,128)(2,1)}) %all-gather.2.cloned.1.call-update) | async-done | bytes 2097168 | tf_op jit(solution)/shard_map/all_gather | solution.py:88
  35.5 4.6 gather_fusion
  40.1 2.8 convert_bitcast_fusion
  43.0 2.6 add_reduce_fusion
  45.6 3.4 convert_bitcast_fusion.1
  48.9 4.7 fusion.91
  53.7 2.0 copy.296
  55.7 2.9 copy.298
  58.6 9.6 %fusion.32 = (bf16[1,512,1024]{2,1,0:T(8,128)(2,1)S(1)}, bf16[1,512,1024]{2,1,0:T(8,128)(2,1)S(1)}) fusion(f32[1,512,1024]{2,0,1:T(1,128)} %bitcast.358, f32[1,512,1024]{2,0,1:T(1,128)S(1)} %bitcast.357, f32[1024]{0:T(1024)S(1)} %add_multiply_fusion, f32[512]{0:T(512)S(1)} %bitcast.441), kind=kLoop, calls=%fused_computation.54 | loop fusion | flops 4718592 | bytes 6297600 | tf_op jit(solution)/shard_map/slice | solution.py:30
  70.3 2.5 collective-permute-start
  74.8 89.2 %collective-permute-done = bf16[2,512,1024]{2,1,0:T(8,128)(2,1)S(1)} collective-permute-done((bf16[2,512,1024]{2,1,0:T(8,128)(2,1)S(1)}, bf16[2,512,1024]{2,1,0:T(8,128)(2,1)S(1)}, u32[]{:S(2)}, u32[]{:S(2)}) %collective-permute-start) | collective-permute-done | bytes 2097184 | tf_op jit(solution)/shard_map/ppermute | solution.py:17
  165.0 8.8 %fusion.42 = (bf16[1,512,1024]{2,1,0:T(8,128)(2,1)S(1)}, bf16[1,512,1024]{2,1,0:T(8,128)(2,1)S(1)}) fusion(f32[2,512,1024]{2,1,0:T(8,128)S(1)} %fusion.56, f32[512]{0:T(512)S(1)} %bitcast.443, f32[1024]{0:T(1024)S(1)} %add_multiply_fusion), kind=kLoop, calls=%fused_computation.64 | loop fusion | flops 4718592 | bytes 6297600 | tf_op jit(solution)/shard_map/slice | solution.py:31
  178.5 44.5 %collective-permute-done.1 = bf16[2,512,1024]{2,1,0:T(8,128)(2,1)S(1)} collective-permute-done((bf16[2,512,1024]{2,1,0:T(8,128)(2,1)S(1)}, bf16[2,512,1024]{2,1,0:T(8,128)(2,1)S(1)}, u32[]{:S(2)}, u32[]{:S(2)}) %collective-permute-start.1) | collective-permute-done | bytes 2097184 | tf_op jit(solution)/shard_map/ppermute | solution.py:17
  224.0 8.4 %fusion.50 = (bf16[1,512,1024]{2,1,0:T(8,128)(2,1)S(1)}, bf16[1,512,1024]{2,1,0:T(8,128)(2,1)S(1)}) fusion(f32[2,512,1024]{2,1,0:T(8,128)S(1)} %fusion.55, f32[512]{0:T(512)S(1)} %bitcast.445, f32[1024]{0:T(1024)S(1)} %add_multiply_fusion), kind=kLoop, calls=%fused_computation.72 | loop fusion | flops 4718592 | bytes 6297600 | tf_op jit(solution)/shard_map/slice | solution.py:31
  234.6 1.5 collective-permute-start.2
  238.1 42.6 %collective-permute-done.2 = bf16[2,512,1024]{2,1,0:T(8,128)(2,1)S(1)} collective-permute-done((bf16[2,512,1024]{2,1,0:T(8,128)(2,1)S(1)}, bf16[2,512,1024]{2,1,0:T(8,128)(2,1)S(1)}, u32[]{:S(2)}, u32[]{:S(2)}) %collective-permute-start.2) | collective-permute-done | bytes 2097184 | tf_op jit(solution)/shard_map/ppermute | solution.py:17
  282.0 1.5 collective-permute-start.3
  285.4 41.7 %collective-permute-done.3 = bf16[2,512,1024]{2,1,0:T(8,128)(2,1)S(1)} collective-permute-done((bf16[2,512,1024]{2,1,0:T(8,128)(2,1)S(1)}, bf16[2,512,1024]{2,1,0:T(8,128)(2,1)S(1)}, u32[]{:S(2)}, u32[]{:S(2)}) %collective-permute-start.3) | collective-permute-done | bytes 2097184 | tf_op jit(solution)/shard_map/ppermute | solution.py:17
  330.4 8.6 %fusion.52 = (bf16[1,512,1024]{2,1,0:T(8,128)(2,1)S(1)}, bf16[1,512,1024]{2,1,0:T(8,128)(2,1)S(1)}) fusion(f32[2,512,1024]{2,1,0:T(8,128)S(1)} %maximum_add_fusion.3, f32[512]{0:T(512)S(1)} %bitcast.446, f32[1024]{0:T(1024)S(1)} %add_multiply_fusion), kind=kLoop, calls=%fused_computation.74 | loop fusion | flops 4718592 | bytes 6297600 | tf_op jit(solution)/shard_map/slice | solution.py:30
  339.3 2.6 collective-permute-start.4
  343.6 41.4 %collective-permute-done.4 = bf16[2,512,1024]{2,1,0:T(8,128)(2,1)S(1)} collective-permute-done((bf16[2,512,1024]{2,1,0:T(8,128)(2,1)S(1)}, bf16[2,512,1024]{2,1,0:T(8,128)(2,1)S(1)}, u32[]{:S(2)}, u32[]{:S(2)}) %collective-permute-start.4) | collective-permute-done | bytes 2097184 | tf_op jit(solution)/shard_map/ppermute | solution.py:17
  388.3 8.4 %fusion.44 = (bf16[1,512,1024]{2,1,0:T(8,128)(2,1)S(1)}, bf16[1,512,1024]{2,1,0:T(8,128)(2,1)S(1)}) fusion(f32[2,512,1024]{2,1,0:T(8,128)S(1)} %maximum_add_fusion.4, f32[512]{0:T(512)S(1)} %bitcast.444, f32[1024]{0:T(1024)S(1)} %add_multiply_fusion), kind=kLoop, calls=%fused_computation.66 | loop fusion | flops 4718592 | bytes 6297600 | tf_op jit(solution)/shard_map/slice | solution.py:30
  396.8 1.5 pad_maximum_fusion.4
  398.3 4.4 collective-permute-start.5
  404.6 85.7 %collective-permute-done.5 = bf16[2,512,1024]{2,1,0:T(8,128)(2,1)} collective-permute-done((bf16[2,512,1024]{2,1,0:T(8,128)(2,1)}, bf16[2,512,1024]{2,1,0:T(8,128)(2,1)}, u32[]{:S(2)}, u32[]{:S(2)}) %collective-permute-start.5) | collective-permute-done | bytes 2097184 | tf_op jit(solution)/shard_map/ppermute | solution.py:17
  490.3 1.7 fusion.92
  495.2 8.5 %fusion.78 = (bf16[64,8,8,128]{3,1,2,0:T(8,128)(2,1)S(1)}, bf16[64,8,8,128]{3,1,2,0:T(8,128)(2,1)S(1)}) fusion(f32[2,512,1024]{2,1,0:T(8,128)S(1)} %maximum_add_fusion.5, f32[1024]{0:T(1024)S(1)} %add_multiply_fusion, f32[512]{0:T(512)S(1)} %bitcast.442), kind=kLoop, calls=%fused_computation.130 | loop fusion | flops 4718592 | bytes 6297600
  506.1 2.8 convert_bitcast_fusion.2
  508.8 2.8 reshape.480
  516.0 1.5 copy.362
  517.5 30.9 %reduce-scatter.4.cloned.1.call-done = bf16[8,32768]{1,0:T(8,128)(2,1)} async-done(((bf16[32,32768]{1,0:T(8,128)(2,1)}), bf16[8,32768]{1,0:T(8,128)(2,1)}) %reduce-scatter.4.cloned.1.call-update) | async-done | bytes 524304
  (117 shorter events, 41.2 us)
Async XLA Ops:
  7.2 38.4 %copy-start = (bf16[128,128]{1,0:T(8,128)(2,1)S(1)}, bf16[128,128]{1,0:T(8,128)(2,1)}, u32[]{:S(2)}) copy-start(bf16[128,128]{1,0:T(8,128)(2,1)} %param.14) | copy-start | bytes 98308
  7.2 2.3 copy-start.9
  7.2 2.6 copy-start.6
  7.2 3.0 copy-start.8
  7.2 3.0 copy-start.4
  7.2 28.3 %all-gather.2.cloned.1.call-start = ((), (), s32[]{:S(2)}) async-start(), calls=%async_computation.1 | async-start | bytes 2621440 | tf_op jit(solution)/shard_map/all_gather | solution.py:88
  9.5 538.9 %reduce-scatter.4.cloned.1.call-start = ((), (), s32[]{:S(2)}) async-start(), calls=%async_computation.2 | async-start | bytes 2621440
  42.9 2.6 copy-start.7
  70.1 2.7 copy-start.5
  70.3 93.7 %collective-permute-start = (bf16[2,512,1024]{2,1,0:T(8,128)(2,1)S(1)}, bf16[2,512,1024]{2,1,0:T(8,128)(2,1)S(1)}, u32[]{:S(2)}, u32[]{:S(2)}) collective-permute-start(bf16[2,512,1024]{2,1,0:T(8,128)(2,1)S(1)} %pad_maximum_fusion), channel_id=1, source_target_pairs={{0,16},{16,0},{4,20},{20,4},{8,24},{24,8},{12,28},{28,12},{1,17},{... | collective-permute-start | bytes 6291464 | tf_op jit(solution)/shard_map/ppermute | solution.py:17
  176.0 47.0 %collective-permute-start.1 = (bf16[2,512,1024]{2,1,0:T(8,128)(2,1)S(1)}, bf16[2,512,1024]{2,1,0:T(8,128)(2,1)S(1)}, u32[]{:S(2)}, u32[]{:S(2)}) collective-permute-start(bf16[2,512,1024]{2,1,0:T(8,128)(2,1)S(1)} %pad_maximum_fusion.1), channel_id=1, source_target_pairs={{0,8},{8,0},{4,12},{12,4},{16,24},{24,16},{20,28},{28,20},{1,9},{9... | collective-permute-start | bytes 6291464 | tf_op jit(solution)/shard_map/ppermute | solution.py:17
  234.6 46.1 %collective-permute-start.2 = (bf16[2,512,1024]{2,1,0:T(8,128)(2,1)S(1)}, bf16[2,512,1024]{2,1,0:T(8,128)(2,1)S(1)}, u32[]{:S(2)}, u32[]{:S(2)}) collective-permute-start(bf16[2,512,1024]{2,1,0:T(8,128)(2,1)S(1)} %pad_maximum_fusion.2), channel_id=1, source_target_pairs={{0,4},{4,0},{8,12},{12,8},{16,20},{20,16},{24,28},{28,24},{1,5},{5... | collective-permute-start | bytes 6291464 | tf_op jit(solution)/shard_map/ppermute | solution.py:17
  237.6 43.1 %copy-start.3 = (bf16[2,512,1024]{2,1,0:T(8,128)(2,1)S(1)}, bf16[2,512,1024]{2,1,0:T(8,128)(2,1)}, u32[]{:S(2)}) copy-start(bf16[2,512,1024]{2,1,0:T(8,128)(2,1)} %param.9) | copy-start | bytes 6291460
  282.0 1.7 copy-start.1
  282.0 45.2 %collective-permute-start.3 = (bf16[2,512,1024]{2,1,0:T(8,128)(2,1)S(1)}, bf16[2,512,1024]{2,1,0:T(8,128)(2,1)S(1)}, u32[]{:S(2)}, u32[]{:S(2)}) collective-permute-start(bf16[2,512,1024]{2,1,0:T(8,128)(2,1)S(1)} %subtract_convert_fusion), channel_id=1, source_target_pairs={{0,4},{4,0},{8,12},{12,8},{16,20},{20,16},{24,28},{28,24},{1,5},{5... | collective-permute-start | bytes 6291464 | tf_op jit(solution)/shard_map/ppermute | solution.py:17
  339.3 45.7 %collective-permute-start.4 = (bf16[2,512,1024]{2,1,0:T(8,128)(2,1)S(1)}, bf16[2,512,1024]{2,1,0:T(8,128)(2,1)S(1)}, u32[]{:S(2)}, u32[]{:S(2)}) collective-permute-start(bf16[2,512,1024]{2,1,0:T(8,128)(2,1)S(1)} %pad_maximum_fusion.3), channel_id=1, source_target_pairs={{0,8},{8,0},{4,12},{12,4},{16,24},{24,16},{20,28},{28,20},{1,9},{9... | collective-permute-start | bytes 6291464 | tf_op jit(solution)/shard_map/ppermute | solution.py:17
  398.3 92.0 %collective-permute-start.5 = (bf16[2,512,1024]{2,1,0:T(8,128)(2,1)}, bf16[2,512,1024]{2,1,0:T(8,128)(2,1)}, u32[]{:S(2)}, u32[]{:S(2)}) collective-permute-start(bf16[2,512,1024]{2,1,0:T(8,128)(2,1)} %pad_maximum_fusion.4), channel_id=1, source_target_pairs={{0,16},{16,0},{4,20},{20,4},{8,24},{24,8},{12,28},{28,12},{1,17},{... | collective-permute-start | bytes 6291464 | tf_op jit(solution)/shard_map/ppermute | solution.py:17
  517.4 32.1 %copy-start.2 = (f32[2,8,128,128]{3,2,1,0:T(8,128)S(1)}, f32[2,8,128,128]{3,2,1,0:T(8,128)}, u32[]{:S(2)}) copy-start(f32[2,8,128,128]{3,2,1,0:T(8,128)} %param.10) | copy-start | bytes 3145732
Sparse Core Ops, SparseCore 0:
  10.2 25.2 all-gather.1
  517.6 30.7 reduce-scatter.3
where the time goes:
time: 567 us; the launch traced here: 558 us
  waiting for transfers between devices  401 us (71%)
  other arithmetic  72.2 us (13%)
  matrix products  32.1 us (6%)
  local copies, waits for them, and re-layouts  24.1 us (4%)
  between operations  15 us (3%)
  starting transfers between devices  13.1 us (2%)
    ppermute x6, waiting for transfers between devices, from_partner(): return lax.ppermute(block, axis, route)  345 us
    unnamed x3, waiting for transfers between devices  30.9 us
    slice x3, other arithmetic, blockwise(): real_real = multiply(blocks[0], values[0])  26.6 us
    all_gather x1, waiting for transfers between devices, per_device(): region = lax.all_gather(image_half, 'tile', axis=1, tiled=True)  25.3 us
    dot_general x48, matrix products, multiply(): jnp.einsum(pattern, left_op, right_op, preferred_element_type=jnp.float32)  21.9 us
    slice x2, other arithmetic, blockwise(): imag_imag = multiply(blocks[1], values[1])  17.2 us
    ppermute x6, starting transfers between devices, from_partner(): return lax.ppermute(block, axis, route)  13 us
  transfers between devices with their start and end apart: 8, of which 8 were waited for; matrix products, arithmetic and copies ran while one was open for 2% of the time, Pallas kernels for 0%

commit v1 on v0

v1 whole, which is shorter than its diff:
```python
import functools

import jax
import jax.numpy as jnp
from jax import lax
from jax.experimental import pallas as pl
from jax.experimental.pallas import tpu as pltpu
from jax.sharding import PartitionSpec as P

step_length = 0.1
f32 = jnp.float32
bf16 = jnp.bfloat16
MESH = pl.DeviceIdType.MESH

LAGS = (0, 2, 3, 4, 5, 6, 8, 9)


def kernel(
    sizes,
    map_ref,
    cos_ref,
    sin_ref,
    echoes_ref,
    image_ref,
    own_ref,
    pair_ref,
    angle_ref,
    turn_ref,
    beam_ref,
    beam_t_ref,
    range_ref,
    range_t_ref,
    weight_ref,
    new_ref,
    residual_ref,
    region,
    back_mat,
    fore_mat,
    phases,
    held,
    sendbuf,
    recvbuf,
    spread,
    total,
    weights,
    mat_sem,
    g_send,
    g_recv,
    w_send,
    w_recv,
    x_send,
    x_recv,
    s_send,
    s_recv,
):
    tiles, chunks, rows_n, side, sections, owned, hits = sizes
    stages = 2 * sections
    me_t = lax.axis_index("tile")
    me_s = lax.axis_index("sub")

    def partner(bit):
        width = 1 << bit
        return me_s + width - 2 * width * ((me_s // width) % 2)

    bits = [sections - 1 - n if n < sections else n - sections for n in range(stages)]

    def mat_copy(which, k, i):
        ref = own_ref if which == 0 else pair_ref
        return pltpu.make_async_copy(
            ref.at[k, :, i], spread.at[me_t, which * sections + k, i], mat_sem.at[which, k, i]
        )

    for which in range(2):
        for k in range(sections):
            for i in range(rows_n):
                mat_copy(which, k, i).start()

    barrier = pltpu.get_barrier_semaphore()
    for d in range(1, tiles):
        pl.semaphore_signal(
            barrier, inc=1, device_id={"tile": (me_t + d) % tiles}, device_id_type=MESH
        )
    for bit in range(sections):
        pl.semaphore_signal(barrier, inc=1, device_id={"sub": partner(bit)}, device_id_type=MESH)

    def convert(u, carry):
        for p in range(2):
            region[me_t * owned + u, p] = image_ref[p, u].astype(bf16)
        return carry

    lax.fori_loop(0, owned, convert, 0)
    pl.semaphore_wait(barrier, tiles - 1 + sections)

    def region_copy(d, src):
        return pltpu.make_async_remote_copy(
            src_ref=region.at[pl.ds(src * owned, owned)],
            dst_ref=region.at[pl.ds(src * owned, owned)],
            send_sem=g_send.at[d],
            recv_sem=g_recv.at[src],
            device_id={"tile": (me_t + d) % tiles},
            device_id_type=MESH,
        )

    def weight_copy(d, src):
        dest = (me_t + d) % tiles
        return pltpu.make_async_remote_copy(
            src_ref=weight_ref.at[dest],
            dst_ref=weights.at[src],
            send_sem=w_send.at[d],
            recv_sem=w_recv.at[src],
            device_id={"tile": dest},
            device_id_type=MESH,
        )

    for d in range(1, tiles):
        region_copy(d, me_t).start()
    for d in range(1, tiles):
        weight_copy(d, me_t).start()
    weights[me_t] = weight_ref[me_t]

    base = lax.convert_element_type(me_t * (chunks * side), f32)
    total_range = tiles * chunks * side
    for k in range(sections):

        def start_phase(i, carry, k=k):
            col = lax.broadcasted_iota(jnp.int32, (side, side), 1).astype(f32)
            rho = (base + col + 0.5) / total_range
            theta = angle_ref[k, i] * rho
            c, s = jnp.cos(theta), jnp.sin(theta)
            phases[sections - 1 - k, 0, i] = c
            phases[sections - 1 - k, 1, i] = s
            phases[sections + k, 0, i] = c
            phases[sections + k, 1, i] = s
            return carry

        lax.fori_loop(0, rows_n, start_phase, 0)

    for k in range(sections):
        for i in range(rows_n):
            for which in range(2):
                mat_copy(which, k, i).wait()

    for k in range(sections):

        def build(i, carry, k=k):
            for which in range(2):
                slot = which * sections + k
                real = spread[me_t, slot, i, 0]
                imag = spread[me_t, slot, i, 1]
                real_t = real.astype(f32).T.astype(bf16)
                imag_t = imag.astype(f32).T.astype(bf16)
                lo = 2 * side * which
                back_mat[k, i, pl.ds(lo, side), pl.ds(0, side)] = real_t
                back_mat[k, i, pl.ds(lo, side), pl.ds(side, side)] = imag_t
                back_mat[k, i, pl.ds(lo + side, side), pl.ds(0, side)] = -imag_t
                back_mat[k, i, pl.ds(lo + side, side), pl.ds(side, side)] = real_t
                fore_mat[k, i, pl.ds(0, side), pl.ds(lo, side)] = real
                fore_mat[k, i, pl.ds(0, side), pl.ds(lo + side, side)] = -imag
                fore_mat[k, i, pl.ds(side, side), pl.ds(lo, side)] = imag
                fore_mat[k, i, pl.ds(side, side), pl.ds(lo + side, side)] = real
            return carry

        lax.fori_loop(0, rows_n, build, 0)

    def zero(u, carry):
        total[u] = jnp.zeros_like(total[u])
        return carry

    lax.fori_loop(0, owned, zero, 0)

    for d in range(1, tiles):
        region_copy(d, (me_t + d) % tiles).wait_recv()
    for d in range(1, tiles):
        weight_copy(d, (me_t + d) % tiles).wait_recv()

    def exchange(n, c):
        return pltpu.make_async_remote_copy(
            src_ref=sendbuf.at[c],
            dst_ref=recvbuf.at[n, c],
            send_sem=x_send.at[n, c],
            recv_sem=x_recv.at[n, c],
            device_id={"sub": partner(bits[n])},
            device_id_type=MESH,
        )

    def dot(a, b):
        return jnp.dot(a, b, preferred_element_type=f32)

    def advance(n, i, k):
        c, s = phases[n, 0, i], phases[n, 1, i]
        dc, ds = turn_ref[0, k, i], turn_ref[1, k, i]
        phases[n, 0, i] = c * dc - s * ds
        phases[n, 1, i] = s * dc + c * ds
        return c, s

    def merge_back(n, c, i, level_real, level_imag):
        k = bits[n]
        pc, ps = advance(n, i, k)
        lr, li = level_real.astype(f32), level_imag.astype(f32)
        turned = jnp.concatenate([pc * lr + ps * li, pc * li - ps * lr], axis=0).astype(bf16)
        out = dot(back_mat[k, i], turned)
        held[c, i] = out[: 2 * side].reshape(2, side, side)
        sendbuf[c, i] = out[2 * side :].astype(bf16).reshape(2, side, side)

    def stage_first(c):
        def body(i, carry):
            real = jnp.zeros((side, side), f32)
            imag = jnp.zeros((side, side), f32)
            for h in range(hits):
                at = (i * chunks + c) * hits + h
                q = map_ref[at]
                cc, ss = cos_ref[at], sin_ref[at]
                pr = region[q, 0].astype(f32)
                pi = region[q, 1].astype(f32)
                real += cc * pr + ss * pi
                imag += cc * pi - ss * pr
            routed = jnp.concatenate([real, imag], axis=0).astype(bf16)
            half = dot(routed, range_t_ref[...]).astype(bf16)
            polar_r = dot(beam_t_ref[...], half[:side]).astype(bf16)
            polar_i = dot(beam_t_ref[...], half[side:]).astype(bf16)
            merge_back(0, c, i, polar_r, polar_i)
            return carry

        lax.fori_loop(0, rows_n, body, 0)
        exchange(0, c).start()

    def stage_back(n, c):
        exchange(n - 1, c).wait()

        def body(i, carry):
            level = (held[c, i] + recvbuf[n - 1, c, i].astype(f32)).astype(bf16)
            merge_back(n, c, i, level[0], level[1])
            return carry

        lax.fori_loop(0, rows_n, body, 0)
        exchange(n, c).start()

    def stage_residual(c):
        n = sections
        exchange(n - 1, c).wait()
        cols = pl.ds(pl.multiple_of(c * side, side), side)

        def body(i, carry):
            rows = pl.ds(pl.multiple_of(i * side, side), side)
            level = (held[c, i] + recvbuf[n - 1, c, i].astype(f32)).astype(bf16)
            res = (level.astype(f32) - echoes_ref[:, rows, cols].astype(f32)).astype(bf16)
            residual_ref[:, rows, cols] = res
            sendbuf[c, i] = res
            return carry

        lax.fori_loop(0, rows_n, body, 0)
        exchange(n, c).start()

    def merge_fore(n, c, i):
        k = bits[n]
        values = jnp.concatenate(
            [
                sendbuf[c, i].reshape(2 * side, side),
                recvbuf[n, c, i].reshape(2 * side, side),
            ],
            axis=0,
        )
        mixed = dot(fore_mat[k, i], values)
        mr, mi = mixed[:side], mixed[side:]
        pc, ps = advance(n, i, k)
        return jnp.concatenate([pc * mr - ps * mi, pc * mi + ps * mr], axis=0).astype(bf16)

    def stage_fore(n, c):
        exchange(n, c).wait()

        def body(i, carry):
            sendbuf[c, i] = merge_fore(n, c, i).reshape(2, side, side)
            return carry

        lax.fori_loop(0, rows_n, body, 0)
        exchange(n + 1, c).start()

    def spread_copy(d, src, c):
        return pltpu.make_async_remote_copy(
            src_ref=spread.at[src, c],
            dst_ref=spread.at[src, c],
            send_sem=s_send.at[d, c],
            recv_sem=s_recv.at[src, c],
            device_id={"tile": (me_t + d) % tiles},
            device_id_type=MESH,
        )

    def stage_last(c):
        n = stages - 1
        exchange(n, c).wait()

        def body(i, carry):
            field = merge_fore(n, c, i)
            beamed = jnp.concatenate(
                [dot(beam_ref[...], field[:side]), dot(beam_ref[...], field[side:])], axis=0
            ).astype(bf16)
            out = dot(beamed, range_ref[...]).astype(bf16)
            spread[me_t, c, i] = out.reshape(2, side, side)
            return carry

        lax.fori_loop(0, rows_n, body, 0)
        for d in range(1, tiles):
            spread_copy(d, me_t, c).start()

    part = 16

    def stage_gather(c):
        for d in range(1, tiles):
            spread_copy(d, (me_t + d) % tiles, c).wait_recv()

        def body(b, carry):
            rows = pl.ds(pl.multiple_of(b * part, part), part)
            reals = [total[u, 0, rows] for u in range(owned)]
            imags = [total[u, 1, rows] for u in range(owned)]

            def add(t, sums):
                reals, imags = list(sums[0]), list(sums[1])
                for i in range(rows_n):
                    sr = spread[t, c, i, 0, rows].astype(f32)
                    si = spread[t, c, i, 1, rows].astype(f32)
                    for u in range(owned):
                        wc = weights[t, 0, c * rows_n + i, pl.ds(u, 1)]
                        ws = weights[t, 1, c * rows_n + i, pl.ds(u, 1)]
                        reals[u] += wc * sr - ws * si
                        imags[u] += wc * si + ws * sr
                return tuple(reals), tuple(imags)

            reals, imags = lax.fori_loop(0, tiles, add, (tuple(reals), tuple(imags)))
            for u in range(owned):
                total[u, 0, rows] = reals[u]
                total[u, 1, rows] = imags[u]
            return carry

        lax.fori_loop(0, side // part, body, 0)

    runs = [stage_first]
    for n in range(1, sections):
        runs.append(functools.partial(stage_back, n))
    runs.append(stage_residual)
    for n in range(sections, stages - 1):
        runs.append(functools.partial(stage_fore, n))
    runs.append(stage_last)
    runs.append(stage_gather)

    def step(t, carry):
        for run, lag in zip(runs, LAGS):
            c = t - lag

            @pl.when((c >= 0) & (c < chunks))
            def _():
                run(c)

        return carry

    lax.fori_loop(0, chunks + LAGS[-1], step, 0)

    def finish(u, carry):
        for p in range(2):
            new_ref[p, u] = image_ref[p, u] - step_length * total[u, p]
        return carry

    lax.fori_loop(0, owned, finish, 0)

    for d in range(1, tiles):
        region_copy(d, me_t).wait_send()
        weight_copy(d, me_t).wait_send()

    def drain(c, carry):
        for d in range(1, tiles):
            spread_copy(d, me_t, c).wait_send()
        return carry

    lax.fori_loop(0, chunks, drain, 0)


def per_device(
    echoes,
    image,
    merge_own,
    merge_pair,
    merge_angle,
    beam_kernel,
    range_kernel,
    block_map,
    route_angle,
):
    side = beam_kernel.shape[0]
    sections = merge_own.shape[0]
    rows_n, chunks, hits = block_map.shape
    tiles = lax.axis_size("tile")
    owned = image.shape[1]
    stages = 2 * sections
    beams = echoes.shape[1]
    total_range = echoes.shape[2] * tiles

    own = merge_own.reshape(sections, 2, rows_n, side, side)
    pair = merge_pair.reshape(sections, 2, rows_n, side, side)
    angle = jnp.broadcast_to(merge_angle[:, :, None], (sections, beams, side)).reshape(
        sections, rows_n, side, side
    )
    delta = merge_angle * (side / total_range)
    turn = jnp.broadcast_to(
        jnp.stack([jnp.cos(delta), jnp.sin(delta)])[..., None], (2, sections, beams, side)
    ).reshape(2, sections, rows_n, side, side)
    route_cos = jnp.cos(route_angle)
    route_sin = jnp.sin(route_angle)
    region_count = tiles * owned
    matched = (block_map[..., None] == jnp.arange(region_count)).astype(f32)
    one = jnp.stack(
        [
            jnp.sum(matched * route_cos[..., None], axis=2),
            jnp.sum(matched * route_sin[..., None], axis=2),
        ]
    )
    one = one.reshape(2, rows_n, chunks, tiles, owned).transpose(3, 0, 2, 1, 4)
    weight = jnp.broadcast_to(
        one.reshape(tiles, 2, chunks * rows_n, owned, 1),
        (tiles, 2, chunks * rows_n, owned, side),
    )
    smem = pl.BlockSpec(memory_space=pltpu.SMEM)
    vmem = pl.BlockSpec(memory_space=pltpu.VMEM)
    hbm = pl.BlockSpec(memory_space=pl.ANY)
    block = (2, side, side)
    dma = pltpu.SemaphoreType.DMA
    return pl.pallas_call(
        functools.partial(kernel, (tiles, chunks, rows_n, side, sections, owned, hits)),
        out_shape=(
            jax.ShapeDtypeStruct(image.shape, f32),
            jax.ShapeDtypeStruct(echoes.shape, bf16),
        ),
        in_specs=[smem] * 3 + [vmem, vmem, hbm, hbm] + [vmem] * 7,
        out_specs=(vmem, vmem),
        scratch_shapes=[
            pltpu.VMEM((region_count,) + block, bf16),
            pltpu.VMEM((sections, rows_n, 4 * side, 2 * side), bf16),
            pltpu.VMEM((sections, rows_n, 2 * side, 4 * side), bf16),
            pltpu.VMEM((stages, 2, rows_n, side, side), f32),
            pltpu.VMEM((chunks, rows_n) + block, f32),
            pltpu.VMEM((chunks, rows_n) + block, bf16),
            pltpu.VMEM((stages, chunks, rows_n) + block, bf16),
            pltpu.VMEM((tiles, chunks, rows_n) + block, bf16),
            pltpu.VMEM((owned,) + block, f32),
            pltpu.VMEM((tiles, 2, chunks * rows_n, owned, side), f32),
            dma((2, sections, rows_n)),
            dma((tiles,)),
            dma((tiles,)),
            dma((tiles,)),
            dma((tiles,)),
            dma((stages, chunks)),
            dma((stages, chunks)),
            dma((tiles, chunks)),
            dma((tiles, chunks)),
        ],
        compiler_params=pltpu.CompilerParams(
            collective_id=0, has_side_effects=True, vmem_limit_bytes=63 * 1024 * 1024
        ),
    )(
        block_map.reshape(-1),
        route_cos.reshape(-1),
        route_sin.reshape(-1),
        echoes,
        image,
        own,
        pair,
        angle,
        turn,
        beam_kernel,
        beam_kernel.T,
        range_kernel,
        range_kernel.T,
        weight,
    )


def solution(mesh):
    return jax.shard_map(
        per_device,
        mesh=mesh,
        in_specs=(
            P(None, "sub", "tile"),
            P(None, ("sub", "tile"), None, None),
            P(None, None, "sub", None),
            P(None, None, "sub", None),
            P(None, "sub"),
            P(),
            P(),
            P("sub", "tile", None),
            P("sub", "tile", None),
        ),
        out_specs=(P(None, ("sub", "tile"), None, None), P(None, "sub", "tile")),
        check_vma=False,
    )
```

time: 567 us -> 296 us (0.52); the launches traced: 558 us -> 293 us
  waiting for transfers between devices: 401 us -> 0 us
  Pallas kernels: 0 us -> 275 us
  other arithmetic: 72.2 us -> 1.59 us
  matrix products: 32.1 us -> 0 us
  between operations: 15 us -> 0.7 us
  starting transfers between devices: 13.1 us -> 0 us
  local copies, waits for them, and re-layouts: 24.1 us -> 15.5 us
    ppermute x6 -> x0, waiting for transfers between devices: 345 us -> none  [from_partner(): return lax.ppermute(block, axis, route)]
    pallas_call x0 -> x1, Pallas kernels: none -> 275 us  [per_device(): pl.pallas_call(functools.partial(kernel, (tiles, chunks, rows_n, side, se...]
    slice x5 -> x0, other arithmetic: 43.9 us -> none  [the longest x3 26.6 us: blockwise(): real_real = multiply(blocks[0], values[0])]
    dot_general x54 -> x0, matrix products: 32.1 us -> none  [the longest x48 21.9 us: multiply(): jnp.einsum(pattern, left_op, right_op, preferred_element_type=jnp.float32)]
    unnamed x3 -> x0, waiting for transfers between devices: 30.9 us -> none
    all_gather x1 -> x0, waiting for transfers between devices: 25.3 us -> none  [per_device(): region = lax.all_gather(image_half, 'tile', axis=1, tiled=True)]
    ppermute x6 -> x0, starting transfers between devices: 13 us -> none  [from_partner(): return lax.ppermute(block, axis, route)]
    slice x10 -> x0, local copies, waits for them, and re-layouts: 12 us -> none  [the longest x2 6.77 us: per_device(): level_f[0]]
  transfers between devices with their start and end apart: 8 -> 0, of which waited for: 8 -> 0; matrix products, arithmetic and copies ran while one was open for 2% -> 0% of each run, Pallas kernels for 0% -> 0%
where the time goes in v1:
time: 296 us; the launch traced here: 293 us
  Pallas kernels  275 us (93%)
  local copies, waits for them, and re-layouts  15.5 us (5%)
    pallas_call x1, Pallas kernels, per_device(): pl.pallas_call(functools.partial(kernel, (tiles, chunks, rows_n, side, se...  275 us
    unnamed x7, local copies, waits for them, and re-layouts  7.46 us

profile of v1, /device:TPU:0, one launch (start us, length us, event | category | flops | bytes accessed | tf_op | source)
XLA Modules:
  0.0 292.8 jit_solution(1546269459171899267)
XLA Ops:
  0.6 0.7 broadcast_in_dim.10
  1.3 0.7 fusion
  2.1 0.1 copy.38
  2.2 0.7 reshape.43.sin_ref
  2.9 0.1 copy.37
  3.0 0.7 reshape.42.cos_ref
  3.6 0.8 copy.36
  4.4 0.6 reshape.41.map_ref
  5.0 0.8 multiply_cosine_fusion
  5.8 0.8 select_reduce_fusion.1
  6.6 1.5 copy.39
  8.1 1.5 copy.40
  9.6 0.1 stack.21
  9.7 0.1 stack.22
  9.8 0.1 copy.41
  9.9 1.1 broadcast_in_dim.11.angle_ref
  11.0 1.3 broadcast_in_dim.14.weight_ref
  12.3 1.6 broadcast_in_dim.12.turn_ref
  14.0 275.1 %shard_map.104 = (f32[2,8,128,128]{3,2,1,0:T(8,128)}, bf16[2,512,1024]{2,1,0:T(8,128)(2,1)}) custom-call(s32[64]{0:T(128)} %reshape.41.map_ref, f32[64]{0:T(128)} %reshape.42.cos_ref, f32[64]{0:T(128)} %reshape.43.sin_ref, bf16[2,512,1024]{2,1,0:T(8,128)(2,1)} %echoes_ref.1, f32[2,8,128,128]{3,2,1,0:T(8,128)} %image_ref.1, ...), custom_call_target="tpu_custom_call" | custom-call | tf_op jit(solution)/shard_map/pallas_call | solution.py:425
  289.0 0.0 copy-start
  289.0 2.4 copy.44
  291.5 0.0 copy-done
  291.5 1.3 copy.45
  (4 shorter events, 0.1 us)
Async XLA Ops:
  289.0 2.5 copy-start

commit v2 on v1

--- a/solution.py
+++ b/solution.py
@@ -12,7 +12,7 @@
 bf16 = jnp.bfloat16
 MESH = pl.DeviceIdType.MESH
 
-LAGS = (0, 2, 3, 4, 5, 6, 8, 9)
+LAGS = (0, 1, 2, 3, 4, 5, 6, 7, 8)
 
 
 def kernel(
@@ -24,15 +24,14 @@
     image_ref,
     own_ref,
     pair_ref,
-    angle_ref,
     turn_ref,
     beam_ref,
-    beam_t_ref,
     range_ref,
-    range_t_ref,
     weight_ref,
     new_ref,
     residual_ref,
+    beam_t_ref,
+    range_t_ref,
     region,
     back_mat,
     fore_mat,
@@ -67,7 +66,7 @@
     def mat_copy(which, k, i):
         ref = own_ref if which == 0 else pair_ref
         return pltpu.make_async_copy(
-            ref.at[k, :, i], spread.at[me_t, which * sections + k, i], mat_sem.at[which, k, i]
+            ref.at[k, :, pl.ds(i * side, side)], spread.at[me_t, which * sections + k, i], mat_sem.at[which, k, i]
         )
 
     for which in range(2):
@@ -91,13 +90,15 @@
     lax.fori_loop(0, owned, convert, 0)
     pl.semaphore_wait(barrier, tiles - 1 + sections)
 
-    def region_copy(d, src):
+    sibling = me_t + 1 - 2 * (me_t % 2)
+
+    def region_copy(d, src, dest):
         return pltpu.make_async_remote_copy(
             src_ref=region.at[pl.ds(src * owned, owned)],
             dst_ref=region.at[pl.ds(src * owned, owned)],
             send_sem=g_send.at[d],
             recv_sem=g_recv.at[src],
-            device_id={"tile": (me_t + d) % tiles},
+            device_id={"tile": dest},
             device_id_type=MESH,
         )
 
@@ -112,11 +113,12 @@
             device_id_type=MESH,
         )
 
-    for d in range(1, tiles):
-        region_copy(d, me_t).start()
-    for d in range(1, tiles):
-        weight_copy(d, me_t).start()
+    for d in range(2, tiles, 2):
+        region_copy(d, me_t, (me_t + d) % tiles).start()
+    region_copy(1, me_t, sibling).start()
     weights[me_t] = weight_ref[me_t]
+    beam_t_ref[...] = beam_ref[...].astype(f32).T.astype(bf16)
+    range_t_ref[...] = range_ref[...].astype(f32).T.astype(bf16)
 
     base = lax.convert_element_type(me_t * (chunks * side), f32)
     total_range = tiles * chunks * side
@@ -125,7 +127,7 @@
         def start_phase(i, carry, k=k):
             col = lax.broadcasted_iota(jnp.int32, (side, side), 1).astype(f32)
             rho = (base + col + 0.5) / total_range
-            theta = angle_ref[k, i] * rho
+            theta = turn_ref[2, k, i] * rho
             c, s = jnp.cos(theta), jnp.sin(theta)
             phases[sections - 1 - k, 0, i] = c
             phases[sections - 1 - k, 1, i] = s
@@ -134,6 +136,11 @@
             return carry
 
         lax.fori_loop(0, rows_n, start_phase, 0)
+
+    for d in range(2, tiles, 2):
+        src = (me_t + d) % tiles
+        region_copy(d, src, src).wait_recv()
+        region_copy(d + 1, src, sibling).start()
 
     for k in range(sections):
         for i in range(rows_n):
@@ -168,10 +175,11 @@
 
     lax.fori_loop(0, owned, zero, 0)
 
+    for d in range(2, tiles, 2):
+        region_copy(d + 1, (sibling + d) % tiles, sibling).wait_recv()
+    region_copy(1, sibling, sibling).wait_recv()
     for d in range(1, tiles):
-        region_copy(d, (me_t + d) % tiles).wait_recv()
-    for d in range(1, tiles):
-        weight_copy(d, (me_t + d) % tiles).wait_recv()
+        weight_copy(d, me_t).start()
 
     def exchange(n, c):
         return pltpu.make_async_remote_copy(
@@ -207,9 +215,8 @@
             real = jnp.zeros((side, side), f32)
             imag = jnp.zeros((side, side), f32)
             for h in range(hits):
-                at = (i * chunks + c) * hits + h
-                q = map_ref[at]
-                cc, ss = cos_ref[at], sin_ref[at]
+                q = map_ref[i, c, h]
+                cc, ss = cos_ref[i, c, h], sin_ref[i, c, h]
                 pr = region[q, 0].astype(f32)
                 pi = region[q, 1].astype(f32)
                 real += cc * pr + ss * pi
@@ -275,13 +282,13 @@
         lax.fori_loop(0, rows_n, body, 0)
         exchange(n + 1, c).start()
 
-    def spread_copy(d, src, c):
+    def spread_copy(d, src, dest, c):
         return pltpu.make_async_remote_copy(
             src_ref=spread.at[src, c],
             dst_ref=spread.at[src, c],
             send_sem=s_send.at[d, c],
             recv_sem=s_recv.at[src, c],
-            device_id={"tile": (me_t + d) % tiles},
+            device_id={"tile": dest},
             device_id_type=MESH,
         )
 
@@ -299,14 +306,27 @@
             return carry
 
         lax.fori_loop(0, rows_n, body, 0)
-        for d in range(1, tiles):
-            spread_copy(d, me_t, c).start()
+        for d in range(2, tiles, 2):
+            spread_copy(d, me_t, (me_t + d) % tiles, c).start()
+        spread_copy(1, me_t, sibling, c).start()
+
+    def stage_relay(c):
+        for d in range(2, tiles, 2):
+            src = (me_t + d) % tiles
+            spread_copy(d, src, src, c).wait_recv()
+            spread_copy(d + 1, src, sibling, c).start()
 
     part = 16
 
     def stage_gather(c):
-        for d in range(1, tiles):
-            spread_copy(d, (me_t + d) % tiles, c).wait_recv()
+        for d in range(2, tiles, 2):
+            spread_copy(d + 1, (sibling + d) % tiles, sibling, c).wait_recv()
+        spread_copy(1, sibling, sibling, c).wait_recv()
+
+        @pl.when(c == 0)
+        def _():
+            for d in range(1, tiles):
+                weight_copy(d, (me_t + d) % tiles).wait_recv()
 
         def body(b, carry):
             rows = pl.ds(pl.multiple_of(b * part, part), part)
@@ -340,6 +360,7 @@
     for n in range(sections, stages - 1):
         runs.append(functools.partial(stage_fore, n))
     runs.append(stage_last)
+    runs.append(stage_relay)
     runs.append(stage_gather)
 
     def step(t, carry):
@@ -362,12 +383,12 @@
     lax.fori_loop(0, owned, finish, 0)
 
     for d in range(1, tiles):
-        region_copy(d, me_t).wait_send()
+        region_copy(d, me_t, sibling).wait_send()
         weight_copy(d, me_t).wait_send()
 
     def drain(c, carry):
         for d in range(1, tiles):
-            spread_copy(d, me_t, c).wait_send()
+            spread_copy(d, me_t, sibling, c).wait_send()
         return carry
 
     lax.fori_loop(0, chunks, drain, 0)
@@ -393,15 +414,11 @@
     beams = echoes.shape[1]
     total_range = echoes.shape[2] * tiles
 
-    own = merge_own.reshape(sections, 2, rows_n, side, side)
-    pair = merge_pair.reshape(sections, 2, rows_n, side, side)
-    angle = jnp.broadcast_to(merge_angle[:, :, None], (sections, beams, side)).reshape(
-        sections, rows_n, side, side
-    )
     delta = merge_angle * (side / total_range)
     turn = jnp.broadcast_to(
-        jnp.stack([jnp.cos(delta), jnp.sin(delta)])[..., None], (2, sections, beams, side)
-    ).reshape(2, sections, rows_n, side, side)
+        jnp.stack([jnp.cos(delta), jnp.sin(delta), merge_angle])[..., None],
+        (3, sections, beams, side),
+    ).reshape(3, sections, rows_n, side, side)
     route_cos = jnp.cos(route_angle)
     route_sin = jnp.sin(route_angle)
     region_count = tiles * owned
@@ -428,9 +445,11 @@
             jax.ShapeDtypeStruct(image.shape, f32),
             jax.ShapeDtypeStruct(echoes.shape, bf16),
         ),
-        in_specs=[smem] * 3 + [vmem, vmem, hbm, hbm] + [vmem] * 7,
+        in_specs=[smem] * 3 + [vmem, vmem, hbm, hbm] + [vmem] * 4,
         out_specs=(vmem, vmem),
         scratch_shapes=[
+            pltpu.VMEM((side, side), bf16),
+            pltpu.VMEM((side, side), bf16),
             pltpu.VMEM((region_count,) + block, bf16),
             pltpu.VMEM((sections, rows_n, 4 * side, 2 * side), bf16),
             pltpu.VMEM((sections, rows_n, 2 * side, 4 * side), bf16),
@@ -455,19 +474,16 @@
             collective_id=0, has_side_effects=True, vmem_limit_bytes=63 * 1024 * 1024
         ),
     )(
-        block_map.reshape(-1),
-        route_cos.reshape(-1),
-        route_sin.reshape(-1),
+        block_map,
+        route_cos,
+        route_sin,
         echoes,
         image,
-        own,
-        pair,
-        angle,
+        merge_own,
+        merge_pair,
         turn,
         beam_kernel,
-        beam_kernel.T,
         range_kernel,
-        range_kernel.T,
         weight,
     )
 

time: 296 us -> 257 us (0.87)
  Pallas kernels: 275 us -> 243 us
  local copies, waits for them, and re-layouts: 15.5 us -> 11.4 us
    pallas_call x1, Pallas kernels: 275 us -> 243 us  [per_device(): pl.pallas_call(functools.partial(kernel, (tiles, chunks, rows_n, side, se...]
    unnamed x7 -> x5, local copies, waits for them, and re-layouts: 7.46 us -> 5.15 us
where the time goes in v2:
time: 257 us
  Pallas kernels  243 us (95%)
  local copies, waits for them, and re-layouts  11.4 us (4%)
    pallas_call x1, Pallas kernels, per_device(): pl.pallas_call(functools.partial(kernel, (tiles, chunks, rows_n, side, se...  243 us
    unnamed x5, local copies, waits for them, and re-layouts  5.15 us

profile of v2, /device:TPU:0, one launch (start us, length us, event | category | flops | bytes accessed | tf_op | source)
XLA Modules:
  0.0 256.6 jit_solution(11296654723413681502)
XLA Ops:
  0.6 0.7 stack.23
  1.3 0.7 copy_sine_fusion
  2.1 0.7 copy.36.cos_ref
  2.8 0.7 copy.37.sin_ref
  3.5 1.4 copy.35.map_ref
  4.9 0.8 multiply_cosine_fusion
  5.7 0.8 select_reduce_fusion.1
  6.5 0.1 stack.25
  6.6 0.1 stack.26
  6.7 0.1 copy.34
  6.8 1.3 broadcast_in_dim.8.weight_ref
  8.1 1.8 broadcast_in_dim.6.turn_ref
  10.0 242.8 %shard_map.104 = (f32[2,8,128,128]{3,2,1,0:T(8,128)}, bf16[2,512,1024]{2,1,0:T(8,128)(2,1)}) custom-call(s32[4,8,2]{2,1,0:T(8,128)} %copy.35.map_ref, f32[4,8,2]{2,1,0:T(8,128)} %copy.36.cos_ref, f32[4,8,2]{2,1,0:T(8,128)} %copy.37.sin_ref, bf16[2,512,1024]{2,1,0:T(8,128)(2,1)} %echoes_ref.1, f32[2,8,128,128]{3,2,1,0:T(8,128)} %image_ref.1, ...), custom_call_target="tpu_custom_call" | custom-call | tf_op jit(solution)/shard_map/pallas_call | solution.py:442
  252.8 0.0 copy-start
  252.8 2.4 copy.42
  255.2 0.0 copy-done
  255.2 1.3 copy.43
  (6 shorter events, 0.1 us)
Async XLA Ops:
  252.8 2.5 copy-start

commit v3 on v2

--- a/solution.py
+++ b/solution.py
@@ -8,6 +8,7 @@
 from jax.sharding import PartitionSpec as P
 
 step_length = 0.1
+PARTS = 2
 f32 = jnp.float32
 bf16 = jnp.bfloat16
 MESH = pl.DeviceIdType.MESH
@@ -18,13 +19,12 @@
 def kernel(
     sizes,
     map_ref,
-    cos_ref,
-    sin_ref,
+    route_ref,
     echoes_ref,
     image_ref,
     own_ref,
     pair_ref,
-    turn_ref,
+    angle_ref,
     beam_ref,
     range_ref,
     weight_ref,
@@ -32,6 +32,7 @@
     residual_ref,
     beam_t_ref,
     range_t_ref,
+    turn_ref,
     region,
     back_mat,
     fore_mat,
@@ -122,34 +123,25 @@
 
     base = lax.convert_element_type(me_t * (chunks * side), f32)
     total_range = tiles * chunks * side
-    for k in range(sections):
-
-        def start_phase(i, carry, k=k):
+
+    def prepare(k):
+        for i in range(rows_n):
+            for which in range(2):
+                mat_copy(which, k, i).wait()
+
+        def build(i, carry):
             col = lax.broadcasted_iota(jnp.int32, (side, side), 1).astype(f32)
             rho = (base + col + 0.5) / total_range
-            theta = turn_ref[2, k, i] * rho
+            row = angle_ref[pl.ds(k * rows_n + i, 1)]
+            delta = row * (side / total_range)
+            theta = jnp.broadcast_to(row, (side, side)).T * rho
+            turn_ref[0, k, i] = jnp.broadcast_to(jnp.cos(delta), (side, side)).T
+            turn_ref[1, k, i] = jnp.broadcast_to(jnp.sin(delta), (side, side)).T
             c, s = jnp.cos(theta), jnp.sin(theta)
             phases[sections - 1 - k, 0, i] = c
             phases[sections - 1 - k, 1, i] = s
             phases[sections + k, 0, i] = c
             phases[sections + k, 1, i] = s
-            return carry
-
-        lax.fori_loop(0, rows_n, start_phase, 0)
-
-    for d in range(2, tiles, 2):
-        src = (me_t + d) % tiles
-        region_copy(d, src, src).wait_recv()
-        region_copy(d + 1, src, sibling).start()
-
-    for k in range(sections):
-        for i in range(rows_n):
-            for which in range(2):
-                mat_copy(which, k, i).wait()
-
-    for k in range(sections):
-
-        def build(i, carry, k=k):
             for which in range(2):
                 slot = which * sections + k
                 real = spread[me_t, slot, i, 0]
@@ -169,6 +161,12 @@
 
         lax.fori_loop(0, rows_n, build, 0)
 
+    prepare(sections - 1)
+    for d in range(2, tiles, 2):
+        src = (me_t + d) % tiles
+        region_copy(d, src, src).wait_recv()
+        region_copy(d + 1, src, sibling).start()
+
     def zero(u, carry):
         total[u] = jnp.zeros_like(total[u])
         return carry
@@ -181,12 +179,15 @@
     for d in range(1, tiles):
         weight_copy(d, me_t).start()
 
-    def exchange(n, c):
+    share = rows_n // PARTS
+
+    def exchange(n, c, part):
+        rows = pl.ds(part * share, share)
         return pltpu.make_async_remote_copy(
-            src_ref=sendbuf.at[c],
-            dst_ref=recvbuf.at[n, c],
-            send_sem=x_send.at[n, c],
-            recv_sem=x_recv.at[n, c],
+            src_ref=sendbuf.at[c, rows],
+            dst_ref=recvbuf.at[n, c, rows],
+            send_sem=x_send.at[n, c, part],
+            recv_sem=x_recv.at[n, c, part],
             device_id={"sub": partner(bits[n])},
             device_id_type=MESH,
         )
@@ -216,7 +217,7 @@
             imag = jnp.zeros((side, side), f32)
             for h in range(hits):
                 q = map_ref[i, c, h]
-                cc, ss = cos_ref[i, c, h], sin_ref[i, c, h]
+                cc, ss = route_ref[0, i, c, h], route_ref[1, i, c, h]
                 pr = region[q, 0].astype(f32)
                 pi = region[q, 1].astype(f32)
                 real += cc * pr + ss * pi
@@ -228,23 +229,24 @@
             merge_back(0, c, i, polar_r, polar_i)
             return carry
 
-        lax.fori_loop(0, rows_n, body, 0)
-        exchange(0, c).start()
+        for part in range(PARTS):
+            lax.fori_loop(part * share, (part + 1) * share, body, 0)
+            exchange(0, c, part).start()
 
     def stage_back(n, c):
-        exchange(n - 1, c).wait()
 
         def body(i, carry):
             level = (held[c, i] + recvbuf[n - 1, c, i].astype(f32)).astype(bf16)
             merge_back(n, c, i, level[0], level[1])
             return carry
 
-        lax.fori_loop(0, rows_n, body, 0)
-        exchange(n, c).start()
+        for part in range(PARTS):
+            exchange(n - 1, c, part).wait()
+            lax.fori_loop(part * share, (part + 1) * share, body, 0)
+            exchange(n, c, part).start()
 
     def stage_residual(c):
         n = sections
-        exchange(n - 1, c).wait()
         cols = pl.ds(pl.multiple_of(c * side, side), side)
 
         def body(i, carry):
@@ -255,8 +257,10 @@
             sendbuf[c, i] = res
             return carry
 
-        lax.fori_loop(0, rows_n, body, 0)
-        exchange(n, c).start()
+        for part in range(PARTS):
+            exchange(n - 1, c, part).wait()
+            lax.fori_loop(part * share, (part + 1) * share, body, 0)
+            exchange(n, c, part).start()
 
     def merge_fore(n, c, i):
         k = bits[n]
@@ -273,14 +277,15 @@
         return jnp.concatenate([pc * mr - ps * mi, pc * mi + ps * mr], axis=0).astype(bf16)
 
     def stage_fore(n, c):
-        exchange(n, c).wait()
 
         def body(i, carry):
             sendbuf[c, i] = merge_fore(n, c, i).reshape(2, side, side)
             return carry
 
-        lax.fori_loop(0, rows_n, body, 0)
-        exchange(n + 1, c).start()
+        for part in range(PARTS):
+            exchange(n, c, part).wait()
+            lax.fori_loop(part * share, (part + 1) * share, body, 0)
+            exchange(n + 1, c, part).start()
 
     def spread_copy(d, src, dest, c):
         return pltpu.make_async_remote_copy(
@@ -294,7 +299,6 @@
 
     def stage_last(c):
         n = stages - 1
-        exchange(n, c).wait()
 
         def body(i, carry):
             field = merge_fore(n, c, i)
@@ -305,7 +309,9 @@
             spread[me_t, c, i] = out.reshape(2, side, side)
             return carry
 
-        lax.fori_loop(0, rows_n, body, 0)
+        for part in range(PARTS):
+            exchange(n, c, part).wait()
+            lax.fori_loop(part * share, (part + 1) * share, body, 0)
         for d in range(2, tiles, 2):
             spread_copy(d, me_t, (me_t + d) % tiles, c).start()
         spread_copy(1, me_t, sibling, c).start()
@@ -316,7 +322,7 @@
             spread_copy(d, src, src, c).wait_recv()
             spread_copy(d + 1, src, sibling, c).start()
 
-    part = 16
+    height = 16
 
     def stage_gather(c):
         for d in range(2, tiles, 2):
@@ -329,7 +335,7 @@
                 weight_copy(d, (me_t + d) % tiles).wait_recv()
 
         def body(b, carry):
-            rows = pl.ds(pl.multiple_of(b * part, part), part)
+            rows = pl.ds(pl.multiple_of(b * height, height), height)
             reals = [total[u, 0, rows] for u in range(owned)]
             imags = [total[u, 1, rows] for u in range(owned)]
 
@@ -351,7 +357,7 @@
                 total[u, 1, rows] = imags[u]
             return carry
 
-        lax.fori_loop(0, side // part, body, 0)
+        lax.fori_loop(0, side // height, body, 0)
 
     runs = [stage_first]
     for n in range(1, sections):
@@ -370,6 +376,13 @@
             @pl.when((c >= 0) & (c < chunks))
             def _():
                 run(c)
+
+            if run is stage_first:
+
+                @pl.when(t == 0)
+                def _():
+                    for k in reversed(range(sections - 1)):
+                        prepare(k)
 
         return carry
 
@@ -411,14 +424,7 @@
     tiles = lax.axis_size("tile")
     owned = image.shape[1]
     stages = 2 * sections
-    beams = echoes.shape[1]
-    total_range = echoes.shape[2] * tiles
-
-    delta = merge_angle * (side / total_range)
-    turn = jnp.broadcast_to(
-        jnp.stack([jnp.cos(delta), jnp.sin(delta), merge_angle])[..., None],
-        (3, sections, beams, side),
-    ).reshape(3, sections, rows_n, side, side)
+
     route_cos = jnp.cos(route_angle)
     route_sin = jnp.sin(route_angle)
     region_count = tiles * owned
@@ -445,11 +451,12 @@
             jax.ShapeDtypeStruct(image.shape, f32),
             jax.ShapeDtypeStruct(echoes.shape, bf16),
         ),
-        in_specs=[smem] * 3 + [vmem, vmem, hbm, hbm] + [vmem] * 4,
+        in_specs=[smem] * 2 + [vmem, vmem, hbm, hbm] + [vmem] * 4,
         out_specs=(vmem, vmem),
         scratch_shapes=[
             pltpu.VMEM((side, side), bf16),
             pltpu.VMEM((side, side), bf16),
+            pltpu.VMEM((2, sections, rows_n, side, side), f32),
             pltpu.VMEM((region_count,) + block, bf16),
             pltpu.VMEM((sections, rows_n, 4 * side, 2 * side), bf16),
             pltpu.VMEM((sections, rows_n, 2 * side, 4 * side), bf16),
@@ -465,8 +472,8 @@
             dma((tiles,)),
             dma((tiles,)),
             dma((tiles,)),
-            dma((stages, chunks)),
-            dma((stages, chunks)),
+            dma((stages, chunks, PARTS)),
+            dma((stages, chunks, PARTS)),
             dma((tiles, chunks)),
             dma((tiles, chunks)),
         ],
@@ -475,13 +482,12 @@
         ),
     )(
         block_map,
-        route_cos,
-        route_sin,
+        jnp.stack([route_cos, route_sin]),
         echoes,
         image,
         merge_own,
         merge_pair,
-        turn,
+        merge_angle.reshape(sections * rows_n, side),
         beam_kernel,
         range_kernel,
         weight,

time: 257 us -> 251 us (0.977)
  Pallas kernels: 243 us -> 240 us
    pallas_call x1, Pallas kernels: 243 us -> 240 us  [per_device(): pl.pallas_call(functools.partial(kernel, (tiles, chunks, rows_n, side, se...]
where the time goes in v3:
time: 251 us
  Pallas kernels  240 us (96%)
  local copies, waits for them, and re-layouts  9.48 us (4%)
    pallas_call x1, Pallas kernels, per_device(): pl.pallas_call(functools.partial(kernel, (tiles, chunks, rows_n, side, se...  240 us
    unnamed x5, local copies, waits for them, and re-layouts  5.14 us

profile of v3, /device:TPU:0, one launch (start us, length us, event | category | flops | bytes accessed | tf_op | source)
XLA Modules:
  0.0 250.8 jit_solution(2366103362809430361)
XLA Ops:
  0.6 1.3 reshape.17.angle_ref
  1.9 0.7 fusion
  2.7 1.4 copy.47.map_ref
  4.0 0.7 copy.48.route_ref
  4.8 0.8 select_reduce_fusion.1
  5.6 0.1 stack.21
  5.7 0.1 stack.22
  5.8 0.1 copy.46
  5.9 1.3 broadcast_in_dim.5.weight_ref
  7.2 239.8 %shard_map.104 = (f32[2,8,128,128]{3,2,1,0:T(8,128)}, bf16[2,512,1024]{2,1,0:T(8,128)(2,1)}) custom-call(s32[4,8,2]{2,1,0:T(8,128)} %copy.47.map_ref, f32[2,4,8,2]{3,2,1,0:T(8,128)} %copy.48.route_ref, bf16[2,512,1024]{2,1,0:T(8,128)(2,1)} %echoes_ref.1, f32[2,8,128,128]{3,2,1,0:T(8,128)} %image_ref.1, bf16[3,2,512,128]{3,2,1,0:T(8,128)(2,1)} %own_ref.1, ...), custom_call_target="tpu_custom_call" | custom-call | tf_op jit(solution)/shard_map/pallas_call | solution.py:448
  247.1 0.0 copy-start
  247.1 2.4 copy.53
  249.5 0.0 copy-done
  249.5 1.3 copy.54
  (3 shorter events, 0.0 us)
Async XLA Ops:
  247.1 2.5 copy-start

commit v4 on v3

--- a/solution.py
+++ b/solution.py
@@ -370,7 +370,8 @@
     runs.append(stage_gather)
 
     def step(t, carry):
-        for run, lag in zip(runs, LAGS):
+        order = list(zip(runs, LAGS))
+        for run, lag in [order[1], order[0]] + order[2:]:
             c = t - lag
 
             @pl.when((c >= 0) & (c < chunks))

time: 251 us -> 248 us (0.988)
  Pallas kernels: 240 us -> 236 us
    pallas_call x1, Pallas kernels: 240 us -> 236 us  [per_device(): pl.pallas_call(functools.partial(kernel, (tiles, chunks, rows_n, side, se...]
where the time goes in v4:
time: 248 us; the launch traced here: 247 us
  Pallas kernels  236 us (95%)
  local copies, waits for them, and re-layouts  9.48 us (4%)
    pallas_call x1, Pallas kernels, per_device(): pl.pallas_call(functools.partial(kernel, (tiles, chunks, rows_n, side, se...  236 us
    unnamed x5, local copies, waits for them, and re-layouts  5.14 us

profile of v4, /device:TPU:0, one launch (start us, length us, event | category | flops | bytes accessed | tf_op | source)
XLA Modules:
  0.0 247.5 jit_solution(1902190850483603024)
XLA Ops:
  0.6 1.3 reshape.17.angle_ref
  1.9 0.7 fusion
  2.7 1.4 copy.47.map_ref
  4.0 0.7 copy.48.route_ref
  4.8 0.8 select_reduce_fusion.1
  5.6 0.1 stack.21
  5.7 0.1 stack.22
  5.8 0.1 copy.46
  5.9 1.3 broadcast_in_dim.5.weight_ref
  7.2 236.5 %shard_map.104 = (f32[2,8,128,128]{3,2,1,0:T(8,128)}, bf16[2,512,1024]{2,1,0:T(8,128)(2,1)}) custom-call(s32[4,8,2]{2,1,0:T(8,128)} %copy.47.map_ref, f32[2,4,8,2]{3,2,1,0:T(8,128)} %copy.48.route_ref, bf16[2,512,1024]{2,1,0:T(8,128)(2,1)} %echoes_ref.1, f32[2,8,128,128]{3,2,1,0:T(8,128)} %image_ref.1, bf16[3,2,512,128]{3,2,1,0:T(8,128)(2,1)} %own_ref.1, ...), custom_call_target="tpu_custom_call" | custom-call | tf_op jit(solution)/shard_map/pallas_call | solution.py:449
  243.7 0.0 copy-start
  243.7 2.4 copy.53
  246.2 0.0 copy-done
  246.2 1.3 copy.54
  (3 shorter events, 0.0 us)
Async XLA Ops:
  243.7 2.5 copy-start
